TPU v7x, 512 devices: a whole 4x8x8 slice. The times are simulated.
512 devices in a mesh: req: 4 (over x), head: 2 (over core), exp: 64 (over z, y).
Axes of the slice: x: 4, y: 8, z: 8, core: 2. Of those that a mesh axis runs over, the one named last changes fastest.
Arguments:
- hidden_acts: bfloat16 [65536, 6, 768], P(('req', 'exp'), None, 'head'), parts along dimension 0, may hold values from -6 to 6
- picks: int32 [65536, 6], P(('req', 'exp')), parts along dimension 0, may hold values from 0 to 127, all different within a row; in each aligned block of 256 rows (0 to 255, 256 to 511, ...) at most 15 rows name the same one
- levels: int32 [65536, 6], P(('req', 'exp')), parts along dimension 0, may hold values from 1 to 1024
- down_weight: bfloat16 [128, 768, 2560], P('exp', None, 'head'), may hold values from -0.21875 to 0.21875
Outputs:
- combined: bfloat16 [65536, 2560], P(('req', 'exp'), 'head'), parts along dimension 0
There are 4 independent parts, one for each index of `req`. A program takes and returns all parts, laid end to end along the dimension named above; an argument that names none is the same for every part. Nothing has to cross between parts.
Inputs may be any that keep to these rules, and one draw needn't show every extreme that they name: `picks`: each row names 6 different experts. In each aligned block of 256 rows (the rows of one device) no expert is named by more than 15 rows; in some block one expert is named by exactly 15.
All inputs are finite; a program needn't handle non-finite values.
Results may differ from a plain program's by a relative error of at most 0.0049.
Values may be sent and summed in bfloat16 or wider, within the bound.
No kernel may reach another device: no remote copies, remote signals or barrier semaphores. Data moves between devices by JAX's collectives and lax.ppermute only.
A program may use at most 64 MiB of HBM per device.

v0:
```python
import jax
import jax.numpy as jnp
from jax import lax
from jax.sharding import PartitionSpec as P


def shards(hidden_acts, picks, levels, down_weight):
    tok_count, top_count = picks.shape
    exp_count = lax.axis_size("exp")
    local_experts = down_weight.shape[0]
    experts_all = local_experts * exp_count
    capacity = min(tok_count, max(2, 5 * tok_count * top_count // (4 * experts_all)))
    flat_picks = picks.reshape(-1)
    onehot = (flat_picks[:, None] == jnp.arange(experts_all, dtype=jnp.int32)[None, :]).astype(
        jnp.int32
    )
    earlier = jnp.cumsum(onehot, axis=0) - onehot
    slot_index = jnp.sum(earlier * onehot, axis=1)
    target = flat_picks * capacity + slot_index
    full_rows = lax.all_gather(hidden_acts, "head", axis=2, tiled=True)
    row_width = full_rows.shape[-1]
    buffer = jnp.zeros((experts_all * capacity, row_width), full_rows.dtype)
    buffer = buffer.at[target].set(full_rows.reshape(-1, row_width))
    outputs = jnp.einsum(
        "sjch,jhd->sjcd",
        lax.all_to_all(
            buffer.reshape(exp_count, local_experts, capacity, row_width),
            "exp",
            split_axis=0,
            concat_axis=0,
            tiled=True,
        ),
        down_weight,
        preferred_element_type=jnp.float32,
    ).astype(jnp.bfloat16)
    returned = lax.all_to_all(outputs, "exp", split_axis=0, concat_axis=0, tiled=True)
    back_rows = returned.reshape(experts_all * capacity, -1)[target]
    pick_weight = levels.astype(jnp.float32) / 1024.0
    summed = jnp.sum(
        back_rows.reshape(tok_count, top_count, -1).astype(jnp.float32) * pick_weight[:, :, None],
        axis=1,
    )
    return summed.astype(jnp.bfloat16)


def solution(mesh):
    placed = (
        P(("req", "exp"), None, "head"),
        P(("req", "exp"), None),
        P(("req", "exp"), None),
        P("exp", None, "head"),
    )
    return jax.shard_map(
        shards, mesh=mesh, in_specs=placed, out_specs=P(("req", "exp"), "head"), check_vma=False
    )
```

profile of v0, /device:TPU:114, one launch (start us, length us, event | category | flops | bytes accessed | tf_op | source)
XLA Modules:
  0.0 367.6 jit_solution(5936023028746895570)
XLA Ops:
  6.5 0.0 copy-start
  6.5 0.0 all-gather.2.cloned.1.call-start
  6.5 0.7 all-gather.2.cloned.1.call-update
  7.3 0.8 copy.25
  8.1 0.1 eq.29
  8.2 0.1 eq.25
  8.4 0.1 copy.27
  8.5 0.3 fusion.5
  8.9 0.1 broadcast_add_fusion
  8.9 0.3 copy.28
  9.2 0.0 copy-done
  9.2 0.1 copy.24
  9.4 0.1 mul.29
  9.5 0.5 fusion.8
  10.1 21.8 %all-gather.2.cloned.1.call-done = bf16[256,6,768]{2,0,1:T(8,128)(2,1)} async-done(((bf16[256,6,384]{2,0,1:T(8,128)(2,1)}), bf16[256,6,768]{2,0,1:T(8,128)(2,1)}) %all-gather.2.cloned.1.call-update) | async-done | bytes 2359312 | tf_op jit(solution)/shard_map/all_gather | solution.py:20
  31.9 3.0 copy.29
  34.9 2.3 reshape.76
  37.2 10.0 %scatter_custom_fusion = bf16[1920,768]{1,0:T(8,128)(2,1)} fusion(s32[1536]{0:T(1024)S(1)} %fusion.10, bf16[1536,768]{1,0:T(8,128)(2,1)} %reshape.76, bf16[]{:T(256)} %constant.6.clone.1), kind=kCustom, calls=%fused_computation.7 | custom fusion | bytes 2949632 | tf_op jit(solution)/shard_map/scatter | solution.py:23
  47.1 3.8 %reshape.61 = bf16[64,2,15,768]{3,2,1,0:T(8,128)(2,1)S(1)} reshape(bf16[1920,768]{1,0:T(8,128)(2,1)} %scatter_custom_fusion) | data formatting | bytes 5898240 | tf_op jit(solution)/shard_map/reshape | solution.py:27
  51.0 2.3 copy.30
  53.3 0.0 copy-start.2
  53.3 83.3 %all_to_all.10 = bf16[64,2,15,768]{3,1,2,0:T(2,128)(2,1)S(1)} all-to-all(bf16[64,2,15,768]{3,1,2,0:T(2,128)(2,1)S(1)} %copy.30), channel_id=1, replica_groups=mesh['req'=4,'head'=2,'exp'=64] {'exp'}, dimensions={0} | all-to-all | bytes 5898240 | tf_op jit(solution)/shard_map/all_to_all | solution.py:26
  136.7 0.0 copy-done.2
  136.7 5.7 %fusion = bf16[64,2,15,1280]{3,0,2,1:T(8,128)(2,1)} fusion(bf16[2,768,1280]{2,1,0:T(8,128)(2,1)S(1)} %copy-done.2, bf16[64,2,15,768]{3,1,2,0:T(2,128)(2,1)S(1)} %all_to_all.10), kind=kOutput, calls=%fused_computation.4 | convolution fusion | flops 3777331200 | bytes 11796480 | tf_op jit(solution)/shard_map/sjch,jhd->sjcd/dot_general | solution.py:24
  142.4 9.6 %copy.32 = bf16[64,2,15,1280]{3,1,2,0:T(2,128)(2,1)} copy(bf16[64,2,15,1280]{3,0,2,1:T(8,128)(2,1)} %fusion) | data formatting | bytes 9830400 | tf_op jit(solution)/shard_map/convert_element_type | solution.py:35
  152.0 0.0 copy-start.1
  152.0 11.6 %all-to-all-start.1 = ((bf16[64,2,15,1280]{3,1,2,0:T(2,128)(2,1)}), bf16[64,2,15,1280]{3,1,2,0:T(2,128)(2,1)}, u32[]{:S(2)}, u32[]{:S(2)}) async-start(bf16[64,2,15,1280]{3,1,2,0:T(2,128)(2,1)} %copy.32), calls=%async_computation.1 | async-start | bytes 9830400 | tf_op jit(solution)/shard_map/all_to_all | solution.py:36
  163.6 0.0 copy-done.1
  163.6 0.1 copy.34
  163.8 155.7 %all-to-all-done.1 = bf16[64,2,15,1280]{3,1,2,0:T(2,128)(2,1)} async-done(((bf16[64,2,15,1280]{3,1,2,0:T(2,128)(2,1)}), bf16[64,2,15,1280]{3,1,2,0:T(2,128)(2,1)}, u32[]{:S(2)}, u32[]{:S(2)}) %all-to-all-start.1) | async-done | bytes 4915232 | tf_op jit(solution)/shard_map/all_to_all | solution.py:36
  319.5 5.9 %copy.33 = bf16[64,2,15,1280]{3,2,1,0:T(8,128)(2,1)} copy(bf16[64,2,15,1280]{3,1,2,0:T(2,128)(2,1)} %all-to-all-done.1) | data formatting | bytes 9830400 | tf_op jit(solution)/shard_map/all_to_all | solution.py:36
  325.4 7.6 %reshape.62 = bf16[1920,1280]{1,0:T(8,128)(2,1)} reshape(bf16[64,2,15,1280]{3,2,1,0:T(8,128)(2,1)} %copy.33) | data formatting | bytes 9830400 | tf_op jit(solution)/shard_map/reshape | solution.py:37
  332.9 12.0 %gather_fusion = bf16[1536,1280]{1,0:T(8,128)(2,1)} fusion(bf16[1920,1280]{1,0:T(8,128)(2,1)} %reshape.62, s32[2048]{0:T(1024)S(1)} %pad_clamp_fusion), kind=kCustom, calls=%fused_computation | custom fusion | bytes 7870464 | tf_op jit(solution)/shard_map/gather | solution.py:37
  345.0 7.7 %reshape.63 = f32[256,6,1280]{2,1,0:T(8,128)} reshape(bf16[1536,1280]{1,0:T(8,128)(2,1)} %gather_fusion) | data formatting | bytes 11796480 | tf_op jit(solution)/shard_map/convert_element_type | solution.py:40
  352.7 8.1 %multiply_reduce_fusion = bf16[256,1280]{1,0:T(8,128)(2,1)} fusion(f32[256,6,1280]{2,1,0:T(8,128)} %reshape.63, f32[256,6]{1,0:T(8,128)S(1)} %copy.34), kind=kLoop, calls=%fused_computation.2 | loop fusion | flops 3604480 | bytes 8525824 | tf_op jit(solution)/shard_map/reduce_sum | solution.py:39
  (6 shorter events, 0.1 us)
Async XLA Ops:
  6.5 2.7 copy-start
  6.5 25.3 %all-gather.2.cloned.1.call-start = ((), (), s32[]{:S(2)}) async-start(), calls=%async_computation.2 | async-start | bytes 3538944 | tf_op jit(solution)/shard_map/all_gather | solution.py:20
  53.3 83.4 %copy-start.2 = (bf16[2,768,1280]{2,1,0:T(8,128)(2,1)S(1)}, bf16[2,768,1280]{2,1,0:T(8,128)(2,1)}, u32[]{:S(2)}) copy-start(bf16[2,768,1280]{2,1,0:T(8,128)(2,1)} %param.7) | copy-start | bytes 11796484
  152.0 11.6 %copy-start.1 = (s32[256,6]{0,1:T(8,128)S(1)}, s32[256,6]{0,1:T(8,128)}, u32[]{:S(2)}) copy-start(s32[256,6]{0,1:T(8,128)} %param.6) | copy-start | bytes 18436
  152.0 167.5 %all-to-all-start.1 = ((bf16[64,2,15,1280]{3,1,2,0:T(2,128)(2,1)}), bf16[64,2,15,1280]{3,1,2,0:T(2,128)(2,1)}, u32[]{:S(2)}, u32[]{:S(2)}) async-start(bf16[64,2,15,1280]{3,1,2,0:T(2,128)(2,1)} %copy.32), calls=%async_computation.1 | async-start | bytes 9830400 | tf_op jit(solution)/shard_map/all_to_all | solution.py:36
Sparse Core Ops, SparseCore 0:
  9.4 22.3 all-gather.1
where the time goes:
time: 368 us
  waiting for transfers between devices  178 us (48%)
  blocking collectives  83.3 us (23%)
  local copies, waits for them, and re-layouts  66.2 us (18%)
  between operations  13.6 us (4%)
  starting transfers between devices  11.6 us (3%)
  other arithmetic  9.04 us (2%)
  matrix products  5.71 us (2%)
    all_to_all x1, waiting for transfers between devices, shards(): lax.all_to_all(outputs, 'exp', split_axis=0, concat_axis=0, tiled=True)  156 us
    all_to_all x1, blocking collectives, shards(): lax.all_to_all(buffer.reshape(exp_count, local_experts, capacity, row_wid...  83.3 us
    all_gather x1, waiting for transfers between devices, shards(): full_rows = lax.all_gather(hidden_acts, 'head', axis=2, tiled=True)  21.8 us
    gather x1, local copies, waits for them, and re-layouts, shards(): back_rows = returned.reshape(experts_all * capacity, -1)[target]  12 us
    all_to_all x1, starting transfers between devices, shards(): lax.all_to_all(outputs, 'exp', split_axis=0, concat_axis=0, tiled=True)  11.6 us
    scatter x1, local copies, waits for them, and re-layouts, shards(): buffer = buffer.at[target].set(full_rows.reshape(-1, row_width))  9.98 us
    convert_element_type x1, local copies, waits for them, and re-layouts, shards(): outputs = jnp.einsum('sjch,jhd->sjcd', lax.all_to_all(buffer.reshape(exp_...  9.64 us
    reduce_sum x1, other arithmetic, shards(): jnp.sum(back_rows.reshape(tok_count, top_count, -1).astype(jnp.float32) *...  8.07 us
  transfers between devices with their start and end apart: 2, of which 2 were waited for; matrix products, arithmetic and copies ran while one was open for 1% of the time, Pallas kernels for 0%

commit v1 on v0

v1 whole, which is shorter than its diff:
```python
import functools

import jax
import jax.numpy as jnp
from jax import lax
from jax.experimental import pallas as pl
from jax.experimental.pallas import tpu as pltpu
from jax.sharding import PartitionSpec as P

WIDE = 8
SLOTS = 16
VMEM = 48 * 1024 * 1024


def route_kernel(pick_ref, hidden_ref, rows_ref, target_ref, *, experts):
    top, tokens = pick_ref.shape
    before = lax.broadcasted_iota(jnp.int32, (tokens, tokens), 0)
    after = lax.broadcasted_iota(jnp.int32, (tokens, tokens), 1)
    earlier = jnp.where(before < after, 1.0, 0.0).astype(jnp.bfloat16)
    named = lax.broadcasted_iota(jnp.int32, (experts, tokens), 0)
    carry = jnp.zeros((experts, 1), jnp.float32)
    target_ref[...] = jnp.full(target_ref.shape, -1, jnp.int32)
    targets = []
    for k in range(top):
        pick = pick_ref[k : k + 1, :]
        onehot = jnp.where(named == pick, 1.0, 0.0)
        count = jnp.dot(
            onehot.astype(jnp.bfloat16), earlier, preferred_element_type=jnp.float32
        )
        slot = jnp.sum(onehot * (count + carry), axis=0, keepdims=True)
        carry = carry + jnp.sum(onehot, axis=1, keepdims=True)
        targets.append(pick * SLOTS + slot.astype(jnp.int32))
        target_ref[k : k + 1, :] = targets[k]
    chunk = 256
    for at in range(0, rows_ref.shape[0], chunk):
        row = at + lax.broadcasted_iota(jnp.int32, (chunk, tokens), 0)
        chosen = jnp.concatenate(
            [jnp.where(row == target, 1.0, 0.0).astype(jnp.bfloat16) for target in targets], axis=1
        )
        rows_ref[at : at + chunk, :] = jnp.dot(
            chosen, hidden_ref[...], preferred_element_type=jnp.float32
        ).astype(jnp.bfloat16)


def route(picks, hidden, experts):
    return pl.pallas_call(
        functools.partial(route_kernel, experts=experts),
        out_shape=(
            jax.ShapeDtypeStruct((experts * SLOTS, hidden.shape[1]), jnp.bfloat16),
            jax.ShapeDtypeStruct((WIDE, picks.shape[1]), jnp.int32),
        ),
        compiler_params=pltpu.CompilerParams(vmem_limit_bytes=VMEM),
        name="route",
    )(picks, hidden)


def expert_kernel(head_ref, own_ref, other_ref, own_w_ref, other_w_ref, out_ref):
    sources, _, depth = own_ref.shape
    for e in range(own_w_ref.shape[0]):
        at = slice(e * SLOTS, (e + 1) * SLOTS)
        own = own_ref[:, at, :].reshape(sources * SLOTS, depth)
        other = other_ref[:, at, :].reshape(sources * SLOTS, depth)
        total = jnp.dot(own, own_w_ref[e, 0], preferred_element_type=jnp.float32)
        total = total + jnp.dot(other, other_w_ref[e, 0], preferred_element_type=jnp.float32)
        out_ref[:, at, :] = total.astype(jnp.bfloat16).reshape(sources, SLOTS, -1)


def run_experts(head, own, other, weight):
    sources, rows, depth = own.shape
    local, _, _, width = weight.shape
    step = 8
    return pl.pallas_call(
        expert_kernel,
        out_shape=jax.ShapeDtypeStruct((sources, rows, width), jnp.bfloat16),
        grid_spec=pltpu.PrefetchScalarGridSpec(
            num_scalar_prefetch=1,
            grid=(sources // step,),
            in_specs=[
                pl.BlockSpec((step, rows, depth), lambda i, h: (i, 0, 0)),
                pl.BlockSpec((step, rows, depth), lambda i, h: (i, 0, 0)),
                pl.BlockSpec((local, 1, depth, width), lambda i, h: (0, h[0], 0, 0)),
                pl.BlockSpec((local, 1, depth, width), lambda i, h: (0, 1 - h[0], 0, 0)),
            ],
            out_specs=pl.BlockSpec((step, rows, width), lambda i, h: (i, 0, 0)),
        ),
        compiler_params=pltpu.CompilerParams(vmem_limit_bytes=VMEM),
        name="experts",
    )(head, own, other, weight, weight)


def combine_kernel(target_ref, level_ref, back_ref, out_ref, high_ref, low_ref, wide_ref):
    tokens, rows = high_ref.shape
    chunk = 256

    @pl.when(pl.program_id(0) == 0)
    def _():
        top = level_ref.shape[0]
        wide_ref[...] = jnp.zeros_like(wide_ref)
        wide_ref[0:top, :] = level_ref[...].astype(jnp.float32)
        level = wide_ref[...].T
        target = target_ref[...].astype(jnp.float32).T.astype(jnp.int32)
        for at in range(0, rows, chunk):
            row = at + lax.broadcasted_iota(jnp.int32, (tokens, chunk), 1)
            gate = jnp.zeros((tokens, chunk), jnp.float32)
            for k in range(top):
                gate = jnp.where(row == target[:, k : k + 1], level[:, k : k + 1], gate)
            high = gate.astype(jnp.bfloat16)
            high_ref[:, at : at + chunk] = high
            low_ref[:, at : at + chunk] = (gate - high.astype(jnp.float32)).astype(jnp.bfloat16)

    back = back_ref[...]
    total = jnp.dot(high_ref[...], back, preferred_element_type=jnp.float32)
    total = total + jnp.dot(low_ref[...], back, preferred_element_type=jnp.float32)
    out_ref[...] = (total * (1.0 / 1024.0)).astype(jnp.bfloat16)


def combine(target, levels, back):
    tokens = levels.shape[1]
    rows, width = back.shape
    tile = 256
    return pl.pallas_call(
        combine_kernel,
        out_shape=jax.ShapeDtypeStruct((tokens, width), jnp.bfloat16),
        grid=(width // tile,),
        in_specs=[
            pl.BlockSpec(target.shape, lambda i: (0, 0)),
            pl.BlockSpec(levels.shape, lambda i: (0, 0)),
            pl.BlockSpec((rows, tile), lambda i: (0, i)),
        ],
        out_specs=pl.BlockSpec((tokens, tile), lambda i: (0, i)),
        scratch_shapes=[
            pltpu.VMEM((tokens, rows), jnp.bfloat16),
            pltpu.VMEM((tokens, rows), jnp.bfloat16),
            pltpu.VMEM((WIDE, tokens), jnp.float32),
        ],
        compiler_params=pltpu.CompilerParams(vmem_limit_bytes=VMEM),
        name="combine",
    )(target, levels, back)


def shards(hidden_acts, picks, levels, down_weight):
    tokens, top = picks.shape
    half = hidden_acts.shape[-1]
    local, _, width = down_weight.shape
    devices = lax.axis_size("exp")
    experts = local * devices
    flat_hidden = jnp.transpose(hidden_acts, (1, 0, 2)).reshape(top * tokens, half)
    rows, target = route(picks.T, flat_hidden, experts)
    own = lax.all_to_all(
        rows.reshape(devices, local * SLOTS, half), "exp", split_axis=0, concat_axis=0, tiled=True
    )
    other = lax.ppermute(own, "head", [(0, 1), (1, 0)])
    head = lax.axis_index("head").astype(jnp.int32).reshape(1)
    outputs = run_experts(head, own, other, down_weight.reshape(local, 2, half, width))
    back = lax.all_to_all(outputs, "exp", split_axis=0, concat_axis=0, tiled=True)
    return combine(target, levels.T, back.reshape(experts * SLOTS, width))


def solution(mesh):
    placed = (
        P(("req", "exp"), None, "head"),
        P(("req", "exp"), None),
        P(("req", "exp"), None),
        P("exp", None, "head"),
    )
    return jax.shard_map(
        shards, mesh=mesh, in_specs=placed, out_specs=P(("req", "exp"), "head"), check_vma=False
    )
```

time: 368 us -> 219 us (0.60)
  the two profiles are of different devices: /device:TPU:114 before, /device:TPU:48 now
where the time goes in v1:
time: 219 us
  blocking collectives  191 us (87%)
  Pallas kernels  20.5 us (9%)
  waiting for transfers between devices  3.37 us (2%)
    all_to_all x1, blocking collectives, shards(): lax.all_to_all(outputs, 'exp', split_axis=0, concat_axis=0, tiled=True)  136 us
    all_to_all x1, blocking collectives, shards(): lax.all_to_all(rows.reshape(devices, local * SLOTS, half), 'exp', split_a...  54.6 us
    pallas_call x1, Pallas kernels, run_experts(): pl.pallas_call(expert_kernel, out_shape=jax.ShapeDtypeStruct((sources, ro...  10.2 us
    pallas_call x1, Pallas kernels, combine(): pl.pallas_call(combine_kernel, out_shape=jax.ShapeDtypeStruct((tokens, wi...  6.59 us
  transfers between devices with their start and end apart: 1, of which 1 were waited for; matrix products, arithmetic and copies ran while one was open for 0% of the time, Pallas kernels for 0%

profile of v1, /device:TPU:48, one launch (start us, length us, event | category | flops | bytes accessed | tf_op | source)
XLA Modules:
  0.0 218.9 jit_solution(5857117228135406651)
XLA Ops:
  0.0 0.0 copy-start
  0.0 1.3 copy-done
  1.3 0.0 copy-start.1
  1.3 0.7 copy-done.1
  2.0 3.7 %route.1 = (bf16[2048,384]{1,0:T(8,128)(2,1)S(1)}, s32[8,256]{1,0:T(8,128)S(1)}) custom-call(s32[6,256]{1,0:T(8,128)S(1)} %bitcast.12, bf16[1536,384]{1,0:T(8,128)(2,1)S(1)} %bitcast.11), custom_call_target="tpu_custom_call" | custom-call | tf_op jit(solution)/shard_map/route/pallas_call | solution.py:46
  5.6 54.6 %all_to_all.10.own_ref = bf16[64,32,384]{2,1,0:T(8,128)(2,1)S(1)} all-to-all(bf16[64,32,384]{2,1,0:T(8,128)(2,1)S(1)} %bitcast.10), channel_id=1, replica_groups=mesh['req'=4,'head'=2,'exp'=64] {'exp'}, dimensions={0} | all-to-all | bytes 3145728 | tf_op jit(solution)/shard_map/all_to_all | solution.py:149
  60.3 1.9 collective-permute-start
  62.2 3.4 %collective-permute-done.other_ref = bf16[64,32,384]{2,1,0:T(8,128)(2,1)S(1)} collective-permute-done((bf16[64,32,384]{2,1,0:T(8,128)(2,1)S(1)}, bf16[64,32,384]{2,1,0:T(8,128)(2,1)S(1)}, u32[]{:S(2)}, u32[]{:S(2)}) %collective-permute-start) | collective-permute-done | bytes 1572896 | tf_op jit(solution)/shard_map/ppermute | solution.py:152
  65.5 10.2 %experts.1 = bf16[64,32,1280]{2,1,0:T(8,128)(2,1)} custom-call(s32[1]{0:T(128)} %bitcast.4.head_ref, bf16[64,32,384]{2,1,0:T(8,128)(2,1)S(1)} %all_to_all.10.own_ref, bf16[64,32,384]{2,1,0:T(8,128)(2,1)S(1)} %collective-permute-done.other_ref, bf16[2,2,384,1280]{3,2,1,0:T(8,128)(2,1)} %bitcast.14, bf16[2,2,384,1280]{3,2,1,0:T(8,128)(2,1)} %bitcast.15), custom_call_target="tpu_custom_call" | custom-call | tf_op jit(solution)/shard_map/experts/pallas_call | solution.py:72
  75.8 0.0 copy-start.2
  75.8 136.5 %all_to_all.11 = bf16[64,32,1280]{2,1,0:T(8,128)(2,1)S(1)} all-to-all(bf16[64,32,1280]{2,1,0:T(8,128)(2,1)} %experts.1), channel_id=1, replica_groups=mesh['req'=4,'head'=2,'exp'=64] {'exp'}, dimensions={0} | all-to-all | bytes 10485760 | tf_op jit(solution)/shard_map/all_to_all | solution.py:155
  212.3 0.0 copy-done.2
  212.3 6.6 %combine.1 = bf16[256,1280]{1,0:T(8,128)(2,1)} custom-call(s32[8,256]{1,0:T(8,128)S(1)} %get-tuple-element.7.target_ref, s32[6,256]{1,0:T(8,128)S(1)} %bitcast.13, bf16[2048,1280]{1,0:T(8,128)(2,1)S(1)} %bitcast.9), custom_call_target="tpu_custom_call" | custom-call | tf_op jit(solution)/shard_map/combine/pallas_call | solution.py:121
Async XLA Ops:
  0.0 1.3 copy-start
  1.3 0.7 copy-start.1
  60.3 5.3 %collective-permute-start = (bf16[64,32,384]{2,1,0:T(8,128)(2,1)S(1)}, bf16[64,32,384]{2,1,0:T(8,128)(2,1)S(1)}, u32[]{:S(2)}, u32[]{:S(2)}) collective-permute-start(bf16[64,32,384]{2,1,0:T(8,128)(2,1)S(1)} %all_to_all.10.own_ref), channel_id=1, source_target_pairs={{0,64},{64,0},{1,65},{65,1},{2,66},{66,2},{3,67},{67,3},{4,68},{68... | collective-permute-start | bytes 4718600 | tf_op jit(solution)/shard_map/ppermute | solution.py:152
  75.8 136.5 %copy-start.2 = (s32[256,6]{0,1:T(8,128)S(1)}, s32[256,6]{0,1:T(8,128)}, u32[]{:S(2)}) copy-start(s32[256,6]{0,1:T(8,128)} %param.6) | copy-start | bytes 18436

commit v2 on v1

v2 whole, which is shorter than its diff:
```python
import functools

import jax
import jax.numpy as jnp
from jax import lax
from jax.experimental import pallas as pl
from jax.experimental.pallas import tpu as pltpu
from jax.sharding import PartitionSpec as P

WIDE = 8
SLOTS = 16
VMEM = 24 * 1024 * 1024
WHOLE = pl.BlockSpec(memory_space=pltpu.VMEM)


def route_kernel(pick_ref, hidden_ref, rows_ref, target_ref, *, experts):
    top, tokens = pick_ref.shape
    before = lax.broadcasted_iota(jnp.int32, (tokens, tokens), 0)
    after = lax.broadcasted_iota(jnp.int32, (tokens, tokens), 1)
    earlier = jnp.where(before < after, 1.0, 0.0).astype(jnp.bfloat16)
    named = lax.broadcasted_iota(jnp.int32, (experts, tokens), 0)
    carry = jnp.zeros((experts, 1), jnp.float32)
    target_ref[...] = jnp.full(target_ref.shape, -1, jnp.int32)
    targets = []
    for k in range(top):
        pick = pick_ref[k : k + 1, :]
        onehot = jnp.where(named == pick, 1.0, 0.0)
        count = jnp.dot(
            onehot.astype(jnp.bfloat16), earlier, preferred_element_type=jnp.float32
        )
        slot = jnp.sum(onehot * (count + carry), axis=0, keepdims=True)
        carry = carry + jnp.sum(onehot, axis=1, keepdims=True)
        targets.append(pick * SLOTS + slot.astype(jnp.int32))
        target_ref[k : k + 1, :] = targets[k]
    chunk = 256
    for at in range(0, rows_ref.shape[0], chunk):
        row = at + lax.broadcasted_iota(jnp.int32, (chunk, tokens), 0)
        chosen = jnp.concatenate(
            [jnp.where(row == target, 1.0, 0.0).astype(jnp.bfloat16) for target in targets], axis=1
        )
        rows_ref[at : at + chunk, :] = jnp.dot(
            chosen, hidden_ref[...], preferred_element_type=jnp.float32
        ).astype(jnp.bfloat16)


def route(picks, hidden, experts):
    return pl.pallas_call(
        functools.partial(route_kernel, experts=experts),
        out_shape=(
            jax.ShapeDtypeStruct((experts * SLOTS, hidden.shape[1]), jnp.bfloat16),
            jax.ShapeDtypeStruct((WIDE, picks.shape[1]), jnp.int32),
        ),
        compiler_params=pltpu.CompilerParams(vmem_limit_bytes=VMEM),
        name="route",
    )(picks, hidden)


def expert_kernel(head_ref, own_ref, other_ref, weight_ref, out_ref):
    sources, _, half = own_ref.shape
    local, _, width = weight_ref.shape
    first = head_ref[0] == 0
    tile = 256
    for e in range(local):
        at = slice(e * SLOTS, (e + 1) * SLOTS)
        own = own_ref[:, at, :].reshape(sources * SLOTS, half)
        other = other_ref[:, at, :].reshape(sources * SLOTS, half)
        whole = jnp.concatenate(
            [jnp.where(first, own, other), jnp.where(first, other, own)], axis=1
        )
        for n in range(0, width, tile):
            total = jnp.dot(
                whole, weight_ref[e, :, n : n + tile], preferred_element_type=jnp.float32
            )
            out_ref[:, at, n : n + tile] = total.astype(jnp.bfloat16).reshape(sources, SLOTS, tile)


def run_experts(head, own, other, weight):
    sources, rows, half = own.shape
    local, depth, width = weight.shape
    return pl.pallas_call(
        expert_kernel,
        out_shape=jax.ShapeDtypeStruct((sources, rows, width), jnp.bfloat16),
        in_specs=[pl.BlockSpec(memory_space=pltpu.SMEM), WHOLE, WHOLE, WHOLE],
        out_specs=WHOLE,
        compiler_params=pltpu.CompilerParams(vmem_limit_bytes=VMEM),
        cost_estimate=pl.CostEstimate(
            flops=2 * sources * rows * depth * width, bytes_accessed=12 << 20, transcendentals=0
        ),
        name="experts",
    )(head, own, other, weight)


def gates_kernel(target_ref, level_ref, gates_ref, wide_ref):
    tokens, rows = gates_ref.shape[1:]
    top = level_ref.shape[0]
    chunk = 256
    wide_ref[...] = jnp.zeros_like(wide_ref)
    wide_ref[0:top, :] = level_ref[...].astype(jnp.float32)
    level = wide_ref[...].T
    target = target_ref[...].astype(jnp.float32).T.astype(jnp.int32)
    for at in range(0, rows, chunk):
        row = at + lax.broadcasted_iota(jnp.int32, (tokens, chunk), 1)
        gate = jnp.zeros((tokens, chunk), jnp.float32)
        for k in range(top):
            gate = jnp.where(row == target[:, k : k + 1], level[:, k : k + 1], gate)
        high = gate.astype(jnp.bfloat16)
        gates_ref[0, :, at : at + chunk] = high
        gates_ref[1, :, at : at + chunk] = (gate - high.astype(jnp.float32)).astype(jnp.bfloat16)


def make_gates(target, levels, rows):
    tokens = levels.shape[1]
    return pl.pallas_call(
        gates_kernel,
        out_shape=jax.ShapeDtypeStruct((2, tokens, rows), jnp.bfloat16),
        in_specs=[WHOLE, WHOLE],
        out_specs=WHOLE,
        scratch_shapes=[pltpu.VMEM((WIDE, tokens), jnp.float32)],
        compiler_params=pltpu.CompilerParams(vmem_limit_bytes=VMEM),
        cost_estimate=pl.CostEstimate(flops=4 << 20, bytes_accessed=8 << 20, transcendentals=0),
        name="gates",
    )(target, levels)


def combine_kernel(gates_ref, back_ref, out_ref):
    tile = 256
    for n in range(0, out_ref.shape[1], tile):
        back = back_ref[:, n : n + tile]
        total = jnp.dot(gates_ref[0], back, preferred_element_type=jnp.float32)
        total = total + jnp.dot(gates_ref[1], back, preferred_element_type=jnp.float32)
        out_ref[:, n : n + tile] = (total * (1.0 / 1024.0)).astype(jnp.bfloat16)


def combine(gates, back):
    return pl.pallas_call(
        combine_kernel,
        out_shape=jax.ShapeDtypeStruct((gates.shape[1], back.shape[1]), jnp.bfloat16),
        in_specs=[WHOLE, WHOLE],
        out_specs=WHOLE,
        compiler_params=pltpu.CompilerParams(vmem_limit_bytes=VMEM),
        name="combine",
    )(gates, back)


def shards(hidden_acts, picks, levels, down_weight):
    tokens, top = picks.shape
    half = hidden_acts.shape[-1]
    local, _, width = down_weight.shape
    devices = lax.axis_size("exp")
    experts = local * devices
    flat_hidden = jnp.transpose(hidden_acts, (1, 0, 2)).reshape(top * tokens, half)
    rows, target = route(picks.T, flat_hidden, experts)
    own = lax.all_to_all(
        rows.reshape(devices, local * SLOTS, half), "exp", split_axis=0, concat_axis=0, tiled=True
    )
    other = lax.ppermute(own, "head", [(0, 1), (1, 0)])
    head = lax.axis_index("head").astype(jnp.int32).reshape(1)
    outputs = run_experts(head, own, other, down_weight)
    back = lax.all_to_all(outputs, "exp", split_axis=0, concat_axis=0, tiled=True)
    gates = make_gates(target, levels.T, experts * SLOTS)
    return combine(gates, back.reshape(experts * SLOTS, width))


def solution(mesh):
    placed = (
        P(("req", "exp"), None, "head"),
        P(("req", "exp"), None),
        P(("req", "exp"), None),
        P("exp", None, "head"),
    )
    return jax.shard_map(
        shards, mesh=mesh, in_specs=placed, out_specs=P(("req", "exp"), "head"), check_vma=False
    )
```

time: 219 us -> 272 us (1.24)
  the two profiles are of different devices: /device:TPU:48 before, /device:TPU:44 now
where the time goes in v2:
time: 272 us
  waiting for transfers between devices  181 us (67%)
  blocking collectives  54.4 us (20%)
  Pallas kernels  17.4 us (6%)
  starting transfers between devices  12.6 us (5%)
  local copies, waits for them, and re-layouts  6.42 us (2%)
    all_to_all x1, waiting for transfers between devices, shards(): lax.all_to_all(outputs, 'exp', split_axis=0, concat_axis=0, tiled=True)  177 us
    all_to_all x1, blocking collectives, shards(): lax.all_to_all(rows.reshape(devices, local * SLOTS, half), 'exp', split_a...  54.4 us
    all_to_all x1, starting transfers between devices, shards(): lax.all_to_all(outputs, 'exp', split_axis=0, concat_axis=0, tiled=True)  10.7 us
    unnamed x10, local copies, waits for them, and re-layouts  6.42 us
    pallas_call x1, Pallas kernels, combine(): pl.pallas_call(combine_kernel, out_shape=jax.ShapeDtypeStruct((gates.shap...  6.19 us
    pallas_call x1, Pallas kernels, run_experts(): pl.pallas_call(expert_kernel, out_shape=jax.ShapeDtypeStruct((sources, ro...  5.63 us
  transfers between devices with their start and end apart: 2, of which 2 were waited for; matrix products, arithmetic and copies ran while one was open for 0% of the time, Pallas kernels for 1%

profile of v2, /device:TPU:44, one launch (start us, length us, event | category | flops | bytes accessed | tf_op | source)
XLA Modules:
  0.0 271.7 jit_solution(6398876529068481540)
XLA Ops:
  0.0 0.0 copy-start.1
  0.0 1.3 copy-done.1
  1.3 0.0 copy-start.2
  1.3 0.7 copy-done.2
  2.0 3.7 %route.1 = (bf16[2048,384]{1,0:T(8,128)(2,1)S(1)}, s32[8,256]{1,0:T(8,128)S(1)}) custom-call(s32[6,256]{1,0:T(8,128)S(1)} %bitcast.10, bf16[1536,384]{1,0:T(8,128)(2,1)S(1)} %bitcast.9), custom_call_target="tpu_custom_call" | custom-call | tf_op jit(solution)/shard_map/route/pallas_call | solution.py:47
  5.6 54.4 %all_to_all.10.own_ref = bf16[64,32,384]{2,1,0:T(8,128)(2,1)S(1)} all-to-all(bf16[64,32,384]{2,1,0:T(8,128)(2,1)S(1)} %bitcast.8), channel_id=1, replica_groups=mesh['req'=4,'head'=2,'exp'=64] {'exp'}, dimensions={0} | all-to-all | bytes 3145728 | tf_op jit(solution)/shard_map/all_to_all | solution.py:153
  60.1 1.9 collective-permute-start
  62.0 3.5 %collective-permute-done.other_ref = bf16[64,32,384]{2,1,0:T(8,128)(2,1)} collective-permute-done((bf16[64,32,384]{2,1,0:T(8,128)(2,1)S(1)}, bf16[64,32,384]{2,1,0:T(8,128)(2,1)}, u32[]{:S(2)}, u32[]{:S(2)}) %collective-permute-start) | collective-permute-done | bytes 1572896 | tf_op jit(solution)/shard_map/ppermute | solution.py:156
  65.5 0.0 copy-start.4
  65.5 2.1 copy-done.4
  67.6 5.6 %experts.1 = bf16[64,32,1280]{2,1,0:T(8,128)(2,1)S(1)} custom-call(s32[1]{0:T(128)} %bitcast.4.head_ref, bf16[64,32,384]{2,1,0:T(8,128)(2,1)S(1)} %all_to_all.10.own_ref, bf16[64,32,384]{2,1,0:T(8,128)(2,1)} %collective-permute-done.other_ref, bf16[2,768,1280]{2,1,0:T(8,128)(2,1)S(1)} %copy-done.4), custom_call_target="tpu_custom_call" | custom-call | flops 4026531840 | bytes 12582912 | tf_op jit(solution)/shard_map/experts/pallas_call | solution.py:80
  73.3 0.0 copy-start
  73.3 2.3 copy-done
  75.6 0.0 copy-start.3
  75.6 10.7 %all-to-all-start.1 = ((bf16[64,32,1280]{2,1,0:T(8,128)(2,1)}), bf16[64,32,1280]{2,1,0:T(8,128)(2,1)}, u32[]{:S(2)}, u32[]{:S(2)}) async-start(bf16[64,32,1280]{2,1,0:T(8,128)(2,1)} %copy-done), calls=%async_computation.1 | async-start | bytes 10485760 | tf_op jit(solution)/shard_map/all_to_all | solution.py:159
  86.3 0.0 copy-done.3
  86.3 2.0 gates.1.gates_ref
  88.3 177.3 %all-to-all-done.1 = bf16[64,32,1280]{2,1,0:T(8,128)(2,1)} async-done(((bf16[64,32,1280]{2,1,0:T(8,128)(2,1)}), bf16[64,32,1280]{2,1,0:T(8,128)(2,1)}, u32[]{:S(2)}, u32[]{:S(2)}) %all-to-all-start.1) | async-done | bytes 5242912 | tf_op jit(solution)/shard_map/all_to_all | solution.py:159
  265.5 6.2 %combine.1 = bf16[256,1280]{1,0:T(8,128)(2,1)} custom-call(bf16[2,256,2048]{2,1,0:T(8,128)(2,1)S(1)} %gates.1.gates_ref, bf16[2048,1280]{1,0:T(8,128)(2,1)} %bitcast.6.back_ref), custom_call_target="tpu_custom_call" | custom-call | tf_op jit(solution)/shard_map/combine/pallas_call | solution.py:135
Async XLA Ops:
  0.0 1.3 copy-start.1
  1.3 0.7 copy-start.2
  60.1 5.4 %collective-permute-start = (bf16[64,32,384]{2,1,0:T(8,128)(2,1)S(1)}, bf16[64,32,384]{2,1,0:T(8,128)(2,1)}, u32[]{:S(2)}, u32[]{:S(2)}) collective-permute-start(bf16[64,32,384]{2,1,0:T(8,128)(2,1)S(1)} %all_to_all.10.own_ref), channel_id=1, source_target_pairs={{0,64},{64,0},{1,65},{65,1},{2,66},{66,2},{3,67},{67,3},{4,68},{68... | collective-permute-start | bytes 4718600 | tf_op jit(solution)/shard_map/ppermute | solution.py:156
  65.5 2.1 copy-start.4
  73.3 2.3 copy-start
  75.6 10.7 %copy-start.3 = (s32[256,6]{0,1:T(8,128)S(1)}, s32[256,6]{0,1:T(8,128)}, u32[]{:S(2)}) copy-start(s32[256,6]{0,1:T(8,128)} %param.6) | copy-start | bytes 18436
  75.6 189.9 %all-to-all-start.1 = ((bf16[64,32,1280]{2,1,0:T(8,128)(2,1)}), bf16[64,32,1280]{2,1,0:T(8,128)(2,1)}, u32[]{:S(2)}, u32[]{:S(2)}) async-start(bf16[64,32,1280]{2,1,0:T(8,128)(2,1)} %copy-done), calls=%async_computation.1 | async-start | bytes 10485760 | tf_op jit(solution)/shard_map/all_to_all | solution.py:159

commit v3 on v2

--- a/solution.py
+++ b/solution.py
@@ -11,6 +11,7 @@
 SLOTS = 16
 VMEM = 24 * 1024 * 1024
 WHOLE = pl.BlockSpec(memory_space=pltpu.VMEM)
+FAR = pl.BlockSpec(memory_space=pltpu.HBM)
 
 
 def route_kernel(pick_ref, hidden_ref, rows_ref, target_ref, *, experts):
@@ -50,6 +51,8 @@
             jax.ShapeDtypeStruct((experts * SLOTS, hidden.shape[1]), jnp.bfloat16),
             jax.ShapeDtypeStruct((WIDE, picks.shape[1]), jnp.int32),
         ),
+        in_specs=[WHOLE, WHOLE],
+        out_specs=(WHOLE, WHOLE),
         compiler_params=pltpu.CompilerParams(vmem_limit_bytes=VMEM),
         name="route",
     )(picks, hidden)
@@ -90,7 +93,9 @@
     )(head, own, other, weight)
 
 
-def gates_kernel(target_ref, level_ref, gates_ref, wide_ref):
+def prepare_kernel(target_ref, level_ref, weight_hbm, gates_ref, weight_ref, wide_ref, sem):
+    copy = pltpu.make_async_copy(weight_hbm, weight_ref, sem)
+    copy.start()
     tokens, rows = gates_ref.shape[1:]
     top = level_ref.shape[0]
     chunk = 256
@@ -106,20 +111,24 @@
         high = gate.astype(jnp.bfloat16)
         gates_ref[0, :, at : at + chunk] = high
         gates_ref[1, :, at : at + chunk] = (gate - high.astype(jnp.float32)).astype(jnp.bfloat16)
+    copy.wait()
 
 
-def make_gates(target, levels, rows):
+def prepare(target, levels, weight, rows):
     tokens = levels.shape[1]
     return pl.pallas_call(
-        gates_kernel,
-        out_shape=jax.ShapeDtypeStruct((2, tokens, rows), jnp.bfloat16),
-        in_specs=[WHOLE, WHOLE],
-        out_specs=WHOLE,
-        scratch_shapes=[pltpu.VMEM((WIDE, tokens), jnp.float32)],
+        prepare_kernel,
+        out_shape=(
+            jax.ShapeDtypeStruct((2, tokens, rows), jnp.bfloat16),
+            jax.ShapeDtypeStruct(weight.shape, jnp.bfloat16),
+        ),
+        in_specs=[WHOLE, WHOLE, FAR],
+        out_specs=(WHOLE, WHOLE),
+        scratch_shapes=[pltpu.VMEM((WIDE, tokens), jnp.float32), pltpu.SemaphoreType.DMA],
         compiler_params=pltpu.CompilerParams(vmem_limit_bytes=VMEM),
         cost_estimate=pl.CostEstimate(flops=4 << 20, bytes_accessed=8 << 20, transcendentals=0),
-        name="gates",
-    )(target, levels)
+        name="prepare",
+    )(target, levels, weight)
 
 
 def combine_kernel(gates_ref, back_ref, out_ref):
@@ -155,9 +164,10 @@
     )
     other = lax.ppermute(own, "head", [(0, 1), (1, 0)])
     head = lax.axis_index("head").astype(jnp.int32).reshape(1)
-    outputs = run_experts(head, own, other, down_weight)
+    gates, weight = prepare(target, levels.T, down_weight, experts * SLOTS)
+    other, gates, weight = lax.optimization_barrier((other, gates, weight))
+    outputs = run_experts(head, own, other, weight)
     back = lax.all_to_all(outputs, "exp", split_axis=0, concat_axis=0, tiled=True)
-    gates = make_gates(target, levels.T, experts * SLOTS)
     return combine(gates, back.reshape(experts * SLOTS, width))
 
 

time: 272 us -> 211 us (0.78)
  the two profiles are of different devices: /device:TPU:44 before, /device:TPU:24 now
where the time goes in v3:
time: 211 us
  blocking collectives  191 us (91%)
  Pallas kernels  13.8 us (7%)
  local copies, waits for them, and re-layouts  4.08 us (2%)
    all_to_all x1, blocking collectives, shards(): lax.all_to_all(outputs, 'exp', split_axis=0, concat_axis=0, tiled=True)  135 us
    all_to_all x1, blocking collectives, shards(): lax.all_to_all(rows.reshape(devices, local * SLOTS, half), 'exp', split_a...  56.4 us
    pallas_call x1, Pallas kernels, run_experts(): pl.pallas_call(expert_kernel, out_shape=jax.ShapeDtypeStruct((sources, ro...  4.23 us
  transfers between devices with their start and end apart: 1, of which 0 were waited for; matrix products, arithmetic and copies ran while one was open for 0% of the time, Pallas kernels for 1%

profile of v3, /device:TPU:24, one launch (start us, length us, event | category | flops | bytes accessed | tf_op | source)
XLA Modules:
  0.0 211.1 jit_solution(16670303309438745997)
XLA Ops:
  0.0 0.0 copy-start.1
  0.0 1.3 copy-done.1
  1.3 0.0 copy-start.2
  1.3 0.7 copy-done.2
  2.0 0.0 copy-start.3
  2.0 3.7 %route.1 = (bf16[2048,384]{1,0:T(8,128)(2,1)S(1)}, s32[8,256]{1,0:T(8,128)S(1)}) custom-call(s32[6,256]{1,0:T(8,128)S(1)} %bitcast.11, bf16[1536,384]{1,0:T(8,128)(2,1)S(1)} %bitcast.10), custom_call_target="tpu_custom_call" | custom-call | tf_op jit(solution)/shard_map/route/pallas_call | solution.py:48
  5.7 56.4 %all_to_all.10.own_ref = bf16[64,32,384]{2,1,0:T(8,128)(2,1)S(1)} all-to-all(bf16[64,32,384]{2,1,0:T(8,128)(2,1)S(1)} %bitcast.9), channel_id=1, replica_groups=mesh['req'=4,'head'=2,'exp'=64] {'exp'}, dimensions={0} | all-to-all | bytes 3145728 | tf_op jit(solution)/shard_map/all_to_all | solution.py:162
  62.1 1.9 collective-permute-start
  64.0 0.0 copy-done.3
  64.0 0.0 copy-start
  64.0 2.1 copy-done
  66.1 2.2 %prepare.1 = (bf16[2,256,2048]{2,1,0:T(8,128)(2,1)S(1)}, bf16[2,768,1280]{2,1,0:T(8,128)(2,1)S(1)}) custom-call(s32[8,256]{1,0:T(8,128)S(1)} %get-tuple-element.13.target_ref, s32[6,256]{1,0:T(8,128)S(1)} %bitcast.12, bf16[2,768,1280]{2,1,0:T(8,128)(2,1)S(1)} %copy-done), custom_call_target="tpu_custom_call" | custom-call | flops 4194304 | bytes 8388608 | tf_op jit(solution)/shard_map/prepare/pallas_call | solution.py:119
  68.4 0.0 collective-permute-done.other_ref
  68.4 4.2 %experts.1 = bf16[64,32,1280]{2,1,0:T(8,128)(2,1)S(1)} custom-call(s32[1]{0:T(128)} %bitcast.5.head_ref, bf16[64,32,384]{2,1,0:T(8,128)(2,1)S(1)} %all_to_all.10.own_ref, bf16[64,32,384]{2,1,0:T(8,128)(2,1)S(1)} %collective-permute-done.other_ref, bf16[2,768,1280]{2,1,0:T(8,128)(2,1)S(1)} %get-tuple-element.18.weight_ref), custom_call_target="tpu_custom_call" | custom-call | flops 4026531840 | bytes 12582912 | tf_op jit(solution)/shard_map/experts/pallas_call | solution.py:83
  72.6 134.7 %all_to_all.11 = bf16[64,32,1280]{2,1,0:T(8,128)(2,1)S(1)} all-to-all(bf16[64,32,1280]{2,1,0:T(8,128)(2,1)S(1)} %experts.1), channel_id=1, replica_groups=mesh['req'=4,'head'=2,'exp'=64] {'exp'}, dimensions={0} | all-to-all | bytes 10485760 | tf_op jit(solution)/shard_map/all_to_all | solution.py:170
  207.3 3.7 %combine.1 = bf16[256,1280]{1,0:T(8,128)(2,1)} custom-call(bf16[2,256,2048]{2,1,0:T(8,128)(2,1)S(1)} %get-tuple-element.16.gates_ref, bf16[2048,1280]{1,0:T(8,128)(2,1)S(1)} %bitcast.8), custom_call_target="tpu_custom_call" | custom-call | tf_op jit(solution)/shard_map/combine/pallas_call | solution.py:144
Async XLA Ops:
  0.0 1.3 copy-start.1
  1.3 0.7 copy-start.2
  2.0 62.0 %copy-start.3 = (s32[256,6]{0,1:T(8,128)S(1)}, s32[256,6]{0,1:T(8,128)}, u32[]{:S(2)}) copy-start(s32[256,6]{0,1:T(8,128)} %param.6) | copy-start | bytes 18436
  62.1 6.3 %collective-permute-start = (bf16[64,32,384]{2,1,0:T(8,128)(2,1)S(1)}, bf16[64,32,384]{2,1,0:T(8,128)(2,1)S(1)}, u32[]{:S(2)}, u32[]{:S(2)}) collective-permute-start(bf16[64,32,384]{2,1,0:T(8,128)(2,1)S(1)} %all_to_all.10.own_ref), channel_id=1, source_target_pairs={{0,64},{64,0},{1,65},{65,1},{2,66},{66,2},{3,67},{67,3},{4,68},{68... | collective-permute-start | bytes 4718600 | tf_op jit(solution)/shard_map/ppermute | solution.py:165
  64.0 2.1 %copy-start = (bf16[2,768,1280]{2,1,0:T(8,128)(2,1)S(1)}, bf16[2,768,1280]{2,1,0:T(8,128)(2,1)}, u32[]{:S(2)}) copy-start(bf16[2,768,1280]{2,1,0:T(8,128)(2,1)} %weight_hbm.1) | copy-start | bytes 11796484

commit v4 on v3

--- a/solution.py
+++ b/solution.py
@@ -14,7 +14,18 @@
 FAR = pl.BlockSpec(memory_space=pltpu.HBM)
 
 
-def route_kernel(pick_ref, hidden_ref, rows_ref, target_ref, *, experts):
+def far(array):
+    return pltpu.with_memory_space_constraint(array, pltpu.HBM)
+
+
+def route_kernel(
+    picks_far, hidden_far, rows_ref, target_ref, pick_ref, hidden_ref, pick_sem, hidden_sem, *, experts
+):
+    pick_copy = pltpu.make_async_copy(picks_far, pick_ref, pick_sem)
+    hidden_copy = pltpu.make_async_copy(hidden_far, hidden_ref, hidden_sem)
+    pick_copy.start()
+    hidden_copy.start()
+    pick_copy.wait()
     top, tokens = pick_ref.shape
     before = lax.broadcasted_iota(jnp.int32, (tokens, tokens), 0)
     after = lax.broadcasted_iota(jnp.int32, (tokens, tokens), 1)
@@ -33,6 +44,7 @@
         carry = carry + jnp.sum(onehot, axis=1, keepdims=True)
         targets.append(pick * SLOTS + slot.astype(jnp.int32))
         target_ref[k : k + 1, :] = targets[k]
+    hidden_copy.wait()
     chunk = 256
     for at in range(0, rows_ref.shape[0], chunk):
         row = at + lax.broadcasted_iota(jnp.int32, (chunk, tokens), 0)
@@ -51,11 +63,17 @@
             jax.ShapeDtypeStruct((experts * SLOTS, hidden.shape[1]), jnp.bfloat16),
             jax.ShapeDtypeStruct((WIDE, picks.shape[1]), jnp.int32),
         ),
-        in_specs=[WHOLE, WHOLE],
+        in_specs=[FAR, FAR],
         out_specs=(WHOLE, WHOLE),
+        scratch_shapes=[
+            pltpu.VMEM(picks.shape, jnp.int32),
+            pltpu.VMEM(hidden.shape, jnp.bfloat16),
+            pltpu.SemaphoreType.DMA,
+            pltpu.SemaphoreType.DMA,
+        ],
         compiler_params=pltpu.CompilerParams(vmem_limit_bytes=VMEM),
         name="route",
-    )(picks, hidden)
+    )(far(picks), far(hidden))
 
 
 def expert_kernel(head_ref, own_ref, other_ref, weight_ref, out_ref):
@@ -128,7 +146,7 @@
         compiler_params=pltpu.CompilerParams(vmem_limit_bytes=VMEM),
         cost_estimate=pl.CostEstimate(flops=4 << 20, bytes_accessed=8 << 20, transcendentals=0),
         name="prepare",
-    )(target, levels, weight)
+    )(target, levels, far(weight))
 
 
 def combine_kernel(gates_ref, back_ref, out_ref):

time: 211 us -> 209 us (level)
  the two profiles are of different devices: /device:TPU:24 before, /device:TPU:54 now
where the time goes in v4:
time: 209 us
  blocking collectives  191 us (91%)
  Pallas kernels  14.8 us (7%)
    all_to_all x1, blocking collectives, shards(): lax.all_to_all(outputs, 'exp', split_axis=0, concat_axis=0, tiled=True)  136 us
    all_to_all x1, blocking collectives, shards(): lax.all_to_all(rows.reshape(devices, local * SLOTS, half), 'exp', split_a...  54.6 us
    pallas_call x1, Pallas kernels, route(): pl.pallas_call(functools.partial(route_kernel, experts=experts), out_shap...  4.76 us
    pallas_call x1, Pallas kernels, run_experts(): pl.pallas_call(expert_kernel, out_shape=jax.ShapeDtypeStruct((sources, ro...  4.23 us
  transfers between devices with their start and end apart: 1, of which 1 were waited for; matrix products, arithmetic and copies ran while one was open for 0% of the time, Pallas kernels for 1%

profile of v4, /device:TPU:54, one launch (start us, length us, event | category | flops | bytes accessed | tf_op | source)
XLA Modules:
  0.0 209.0 jit_solution(4544068729926591797)
XLA Ops:
  0.0 0.0 copy-start
  0.0 4.8 %route.1 = (bf16[2048,384]{1,0:T(8,128)(2,1)S(1)}, s32[8,256]{1,0:T(8,128)S(1)}) custom-call(s32[6,256]{1,0:T(8,128)} %bitcast.12, bf16[1536,384]{1,0:T(8,128)(2,1)} %bitcast.11), custom_call_target="tpu_custom_call" | custom-call | tf_op jit(solution)/shard_map/route/pallas_call | solution.py:60
  4.8 54.6 %all_to_all.10.own_ref = bf16[64,32,384]{2,1,0:T(8,128)(2,1)S(1)} all-to-all(bf16[64,32,384]{2,1,0:T(8,128)(2,1)S(1)} %bitcast.9), channel_id=1, replica_groups=mesh['req'=4,'head'=2,'exp'=64] {'exp'}, dimensions={0} | all-to-all | bytes 3145728 | tf_op jit(solution)/shard_map/all_to_all | solution.py:180
  59.4 1.9 collective-permute-start
  61.3 0.0 copy-done
  61.3 2.1 %prepare.1 = (bf16[2,256,2048]{2,1,0:T(8,128)(2,1)S(1)}, bf16[2,768,1280]{2,1,0:T(8,128)(2,1)S(1)}) custom-call(s32[8,256]{1,0:T(8,128)S(1)} %get-tuple-element.13.target_ref, s32[6,256]{1,0:T(8,128)S(1)} %bitcast.10, bf16[2,768,1280]{2,1,0:T(8,128)(2,1)} %weight_hbm.1), custom_call_target="tpu_custom_call" | custom-call | flops 4194304 | bytes 8388608 | tf_op jit(solution)/shard_map/prepare/pallas_call | solution.py:137
  63.4 1.2 collective-permute-done.other_ref
  64.7 4.2 %experts.1 = bf16[64,32,1280]{2,1,0:T(8,128)(2,1)S(1)} custom-call(s32[1]{0:T(128)} %bitcast.5.head_ref, bf16[64,32,384]{2,1,0:T(8,128)(2,1)S(1)} %all_to_all.10.own_ref, bf16[64,32,384]{2,1,0:T(8,128)(2,1)S(1)} %collective-permute-done.other_ref, bf16[2,768,1280]{2,1,0:T(8,128)(2,1)S(1)} %get-tuple-element.18.weight_ref), custom_call_target="tpu_custom_call" | custom-call | flops 4026531840 | bytes 12582912 | tf_op jit(solution)/shard_map/experts/pallas_call | solution.py:101
  68.9 136.4 %all_to_all.11 = bf16[64,32,1280]{2,1,0:T(8,128)(2,1)S(1)} all-to-all(bf16[64,32,1280]{2,1,0:T(8,128)(2,1)S(1)} %experts.1), channel_id=1, replica_groups=mesh['req'=4,'head'=2,'exp'=64] {'exp'}, dimensions={0} | all-to-all | bytes 10485760 | tf_op jit(solution)/shard_map/all_to_all | solution.py:188
  205.3 3.7 %combine.1 = bf16[256,1280]{1,0:T(8,128)(2,1)} custom-call(bf16[2,256,2048]{2,1,0:T(8,128)(2,1)S(1)} %get-tuple-element.16.gates_ref, bf16[2048,1280]{1,0:T(8,128)(2,1)S(1)} %bitcast.8), custom_call_target="tpu_custom_call" | custom-call | tf_op jit(solution)/shard_map/combine/pallas_call | solution.py:162
Async XLA Ops:
  0.0 61.3 %copy-start = (s32[256,6]{0,1:T(8,128)S(1)}, s32[256,6]{0,1:T(8,128)}, u32[]{:S(2)}) copy-start(s32[256,6]{0,1:T(8,128)} %param.6) | copy-start | bytes 18436
  59.4 5.3 %collective-permute-start = (bf16[64,32,384]{2,1,0:T(8,128)(2,1)S(1)}, bf16[64,32,384]{2,1,0:T(8,128)(2,1)S(1)}, u32[]{:S(2)}, u32[]{:S(2)}) collective-permute-start(bf16[64,32,384]{2,1,0:T(8,128)(2,1)S(1)} %all_to_all.10.own_ref), channel_id=1, source_target_pairs={{0,64},{64,0},{1,65},{65,1},{2,66},{66,2},{3,67},{67,3},{4,68},{68... | collective-permute-start | bytes 4718600 | tf_op jit(solution)/shard_map/ppermute | solution.py:183

commit v5 on v4

--- a/solution.py
+++ b/solution.py
@@ -7,6 +7,7 @@
 from jax.experimental.pallas import tpu as pltpu
 from jax.sharding import PartitionSpec as P
 
+LANES = 128
 WIDE = 8
 SLOTS = 16
 VMEM = 24 * 1024 * 1024
@@ -78,29 +79,50 @@
 
 def expert_kernel(head_ref, own_ref, other_ref, weight_ref, out_ref):
     sources, _, half = own_ref.shape
-    local, _, width = weight_ref.shape
+    width = weight_ref.shape[2]
     first = head_ref[0] == 0
-    tile = 256
-    for e in range(local):
+    last_row = lax.broadcasted_iota(jnp.int32, (sources, SLOTS, LANES), 1) == SLOTS - 1
+    tile = 2 * LANES
+    parts = width // tile
+
+    def halves(e):
         at = slice(e * SLOTS, (e + 1) * SLOTS)
         own = own_ref[:, at, :].reshape(sources * SLOTS, half)
         other = other_ref[:, at, :].reshape(sources * SLOTS, half)
-        whole = jnp.concatenate(
+        return jnp.concatenate(
             [jnp.where(first, own, other), jnp.where(first, other, own)], axis=1
         )
-        for n in range(0, width, tile):
-            total = jnp.dot(
-                whole, weight_ref[e, :, n : n + tile], preferred_element_type=jnp.float32
-            )
-            out_ref[:, at, n : n + tile] = total.astype(jnp.bfloat16).reshape(sources, SLOTS, tile)
+
+    def product(whole, e, n):
+        total = jnp.dot(
+            whole, weight_ref[e, :, n * tile : (n + 1) * tile], preferred_element_type=jnp.float32
+        )
+        return [total[:, i * LANES : (i + 1) * LANES].reshape(sources, SLOTS, LANES) for i in (0, 1)]
+
+    def put(j, block):
+        if j < SLOTS - 1:
+            block = jnp.where(last_row, folded[:, j : j + 1, :], block)
+        out_ref[:, :, j * LANES : (j + 1) * LANES] = block.astype(jnp.bfloat16)
+
+    whole = halves(1)
+    left, folded = product(whole, 1, parts - 1)
+    put(4 * parts - 2, left)
+    for n in range(parts - 1):
+        for i, block in enumerate(product(whole, 1, n)):
+            put(2 * (parts + n) + i, block)
+    whole = halves(0)
+    for n in range(parts):
+        for i, block in enumerate(product(whole, 0, n)):
+            put(2 * n + i, block)
 
 
 def run_experts(head, own, other, weight):
     sources, rows, half = own.shape
     local, depth, width = weight.shape
+    assert local == 2 and width % (2 * LANES) == 0 and 2 * width >= SLOTS * LANES
     return pl.pallas_call(
         expert_kernel,
-        out_shape=jax.ShapeDtypeStruct((sources, rows, width), jnp.bfloat16),
+        out_shape=jax.ShapeDtypeStruct((sources, SLOTS, 2 * width - LANES), jnp.bfloat16),
         in_specs=[pl.BlockSpec(memory_space=pltpu.SMEM), WHOLE, WHOLE, WHOLE],
         out_specs=WHOLE,
         compiler_params=pltpu.CompilerParams(vmem_limit_bytes=VMEM),
@@ -120,7 +142,11 @@
     wide_ref[...] = jnp.zeros_like(wide_ref)
     wide_ref[0:top, :] = level_ref[...].astype(jnp.float32)
     level = wide_ref[...].T
-    target = target_ref[...].astype(jnp.float32).T.astype(jnp.int32)
+    row_of = target_ref[...]
+    row_of = (
+        ((row_of // SLOTS) % 2) * (rows // 2) + (row_of // (2 * SLOTS)) * SLOTS + row_of % SLOTS
+    )
+    target = row_of.astype(jnp.float32).T.astype(jnp.int32)
     for at in range(0, rows, chunk):
         row = at + lax.broadcasted_iota(jnp.int32, (tokens, chunk), 1)
         gate = jnp.zeros((tokens, chunk), jnp.float32)
@@ -150,18 +176,41 @@
 
 
 def combine_kernel(gates_ref, back_ref, out_ref):
-    tile = 256
-    for n in range(0, out_ref.shape[1], tile):
-        back = back_ref[:, n : n + tile]
-        total = jnp.dot(gates_ref[0], back, preferred_element_type=jnp.float32)
-        total = total + jnp.dot(gates_ref[1], back, preferred_element_type=jnp.float32)
+    sources, _, lanes = back_ref.shape
+    width = out_ref.shape[1]
+    rows = sources * SLOTS
+    tile = 2 * LANES
+    row = lax.broadcasted_iota(jnp.int32, (sources, SLOTS, LANES), 1)
+    unfolded = jnp.zeros((sources, SLOTS, LANES), jnp.float32)
+    for j in range(SLOTS - 1):
+        block = back_ref[:, :, j * LANES : (j + 1) * LANES].astype(jnp.float32)
+        unfolded = jnp.where(row == j, block[:, SLOTS - 1 : SLOTS, :], unfolded)
+    unfolded = unfolded.astype(jnp.bfloat16).reshape(rows, LANES)
+
+    def gated(e, back):
+        at = slice(e * rows, (e + 1) * rows)
+        high = jnp.dot(gates_ref[0, :, at], back, preferred_element_type=jnp.float32)
+        return high + jnp.dot(gates_ref[1, :, at], back, preferred_element_type=jnp.float32)
+
+    for n in range(0, width, tile):
+        first = back_ref[:, :, n : n + tile].reshape(rows, tile)
+        at = width + n
+        if at + tile <= lanes:
+            second = back_ref[:, :, at : at + tile].reshape(rows, tile)
+        else:
+            second = jnp.concatenate(
+                [back_ref[:, :, at : at + LANES].reshape(rows, LANES), unfolded], axis=1
+            )
+        total = gated(0, first) + gated(1, second)
         out_ref[:, n : n + tile] = (total * (1.0 / 1024.0)).astype(jnp.bfloat16)
 
 
 def combine(gates, back):
     return pl.pallas_call(
         combine_kernel,
-        out_shape=jax.ShapeDtypeStruct((gates.shape[1], back.shape[1]), jnp.bfloat16),
+        out_shape=jax.ShapeDtypeStruct(
+            (gates.shape[1], (back.shape[2] + LANES) // 2), jnp.bfloat16
+        ),
         in_specs=[WHOLE, WHOLE],
         out_specs=WHOLE,
         compiler_params=pltpu.CompilerParams(vmem_limit_bytes=VMEM),
@@ -186,7 +235,7 @@
     other, gates, weight = lax.optimization_barrier((other, gates, weight))
     outputs = run_experts(head, own, other, weight)
     back = lax.all_to_all(outputs, "exp", split_axis=0, concat_axis=0, tiled=True)
-    return combine(gates, back.reshape(experts * SLOTS, width))
+    return combine(gates, back)
 
 
 def solution(mesh):

time: 209 us -> 203 us (0.971)
  the two profiles are of different devices: /device:TPU:54 before, /device:TPU:34 now
where the time goes in v5:
time: 203 us
  blocking collectives  185 us (91%)
  Pallas kernels  15 us (7%)
    all_to_all x1, blocking collectives, shards(): lax.all_to_all(outputs, 'exp', split_axis=0, concat_axis=0, tiled=True)  130 us
    all_to_all x1, blocking collectives, shards(): lax.all_to_all(rows.reshape(devices, local * SLOTS, half), 'exp', split_a...  54.9 us
    pallas_call x1, Pallas kernels, route(): pl.pallas_call(functools.partial(route_kernel, experts=experts), out_shap...  4.76 us
    pallas_call x1, Pallas kernels, run_experts(): pl.pallas_call(expert_kernel, out_shape=jax.ShapeDtypeStruct((sources, SL...  4.23 us
  transfers between devices with their start and end apart: 1, of which 1 were waited for; matrix products, arithmetic and copies ran while one was open for 0% of the time, Pallas kernels for 1%

profile of v5, /device:TPU:34, one launch (start us, length us, event | category | flops | bytes accessed | tf_op | source)
XLA Modules:
  0.0 203.1 jit_solution(5764422346073690045)
XLA Ops:
  0.0 0.0 copy-start
  0.0 4.8 %route.1 = (bf16[2048,384]{1,0:T(8,128)(2,1)S(1)}, s32[8,256]{1,0:T(8,128)S(1)}) custom-call(s32[6,256]{1,0:T(8,128)} %bitcast.10, bf16[1536,384]{1,0:T(8,128)(2,1)} %bitcast.9), custom_call_target="tpu_custom_call" | custom-call | tf_op jit(solution)/shard_map/route/pallas_call | solution.py:61
  4.8 54.9 %all_to_all.10.own_ref = bf16[64,32,384]{2,1,0:T(8,128)(2,1)S(1)} all-to-all(bf16[64,32,384]{2,1,0:T(8,128)(2,1)S(1)} %bitcast.7), channel_id=1, replica_groups=mesh['req'=4,'head'=2,'exp'=64] {'exp'}, dimensions={0} | all-to-all | bytes 3145728 | tf_op jit(solution)/shard_map/all_to_all | solution.py:229
  59.7 1.9 collective-permute-start
  61.6 0.0 copy-done
  61.6 2.1 %prepare.1 = (bf16[2,256,2048]{2,1,0:T(8,128)(2,1)S(1)}, bf16[2,768,1280]{2,1,0:T(8,128)(2,1)S(1)}) custom-call(s32[8,256]{1,0:T(8,128)S(1)} %get-tuple-element.13.target_ref, s32[6,256]{1,0:T(8,128)S(1)} %bitcast.8, bf16[2,768,1280]{2,1,0:T(8,128)(2,1)} %weight_hbm.1), custom_call_target="tpu_custom_call" | custom-call | flops 4194304 | bytes 8388608 | tf_op jit(solution)/shard_map/prepare/pallas_call | solution.py:163
  63.7 1.2 collective-permute-done.other_ref
  65.0 4.2 %experts.1 = bf16[64,16,2432]{2,1,0:T(8,128)(2,1)S(1)} custom-call(s32[1]{0:T(128)} %bitcast.5.head_ref, bf16[64,32,384]{2,1,0:T(8,128)(2,1)S(1)} %all_to_all.10.own_ref, bf16[64,32,384]{2,1,0:T(8,128)(2,1)S(1)} %collective-permute-done.other_ref, bf16[2,768,1280]{2,1,0:T(8,128)(2,1)S(1)} %get-tuple-element.18.weight_ref), custom_call_target="tpu_custom_call" | custom-call | flops 4026531840 | bytes 12582912 | tf_op jit(solution)/shard_map/experts/pallas_call | solution.py:123
  69.2 130.0 %all_to_all.11.back_ref = bf16[64,16,2432]{2,1,0:T(8,128)(2,1)S(1)} all-to-all(bf16[64,16,2432]{2,1,0:T(8,128)(2,1)S(1)} %experts.1), channel_id=1, replica_groups=mesh['req'=4,'head'=2,'exp'=64] {'exp'}, dimensions={0} | all-to-all | bytes 9961472 | tf_op jit(solution)/shard_map/all_to_all | solution.py:237
  199.2 3.9 %combine.1 = bf16[256,1280]{1,0:T(8,128)(2,1)} custom-call(bf16[2,256,2048]{2,1,0:T(8,128)(2,1)S(1)} %get-tuple-element.16.gates_ref, bf16[64,16,2432]{2,1,0:T(8,128)(2,1)S(1)} %all_to_all.11.back_ref), custom_call_target="tpu_custom_call" | custom-call | tf_op jit(solution)/shard_map/combine/pallas_call | solution.py:209
Async XLA Ops:
  0.0 61.6 %copy-start = (s32[256,6]{0,1:T(8,128)S(1)}, s32[256,6]{0,1:T(8,128)}, u32[]{:S(2)}) copy-start(s32[256,6]{0,1:T(8,128)} %param.6) | copy-start | bytes 18436
  59.7 5.3 %collective-permute-start = (bf16[64,32,384]{2,1,0:T(8,128)(2,1)S(1)}, bf16[64,32,384]{2,1,0:T(8,128)(2,1)S(1)}, u32[]{:S(2)}, u32[]{:S(2)}) collective-permute-start(bf16[64,32,384]{2,1,0:T(8,128)(2,1)S(1)} %all_to_all.10.own_ref), channel_id=1, source_target_pairs={{0,64},{64,0},{1,65},{65,1},{2,66},{66,2},{3,67},{67,3},{4,68},{68... | collective-permute-start | bytes 4718600 | tf_op jit(solution)/shard_map/ppermute | solution.py:232

commit v6 on v5

--- a/solution.py
+++ b/solution.py
@@ -8,11 +8,25 @@
 from jax.sharding import PartitionSpec as P
 
 LANES = 128
+RING = 8
+STRIDE = 3
 WIDE = 8
 SLOTS = 16
 VMEM = 24 * 1024 * 1024
 WHOLE = pl.BlockSpec(memory_space=pltpu.VMEM)
 FAR = pl.BlockSpec(memory_space=pltpu.HBM)
+
+
+def placed(expert):
+    device, own = expert // 2, expert % 2
+    return (device // RING * RING + device * STRIDE % RING) * 2 + own
+
+
+def exchange(array):
+    order = [z + y * STRIDE % RING for z in range(0, array.shape[0], RING) for y in range(RING)]
+    return lax.all_to_all(
+        array, "exp", split_axis=0, concat_axis=0, tiled=True, axis_index_groups=[order]
+    )
 
 
 def far(array):
@@ -43,7 +57,7 @@
         )
         slot = jnp.sum(onehot * (count + carry), axis=0, keepdims=True)
         carry = carry + jnp.sum(onehot, axis=1, keepdims=True)
-        targets.append(pick * SLOTS + slot.astype(jnp.int32))
+        targets.append(placed(pick) * SLOTS + slot.astype(jnp.int32))
         target_ref[k : k + 1, :] = targets[k]
     hidden_copy.wait()
     chunk = 256
@@ -226,15 +240,13 @@
     experts = local * devices
     flat_hidden = jnp.transpose(hidden_acts, (1, 0, 2)).reshape(top * tokens, half)
     rows, target = route(picks.T, flat_hidden, experts)
-    own = lax.all_to_all(
-        rows.reshape(devices, local * SLOTS, half), "exp", split_axis=0, concat_axis=0, tiled=True
-    )
+    own = exchange(rows.reshape(devices, local * SLOTS, half))
     other = lax.ppermute(own, "head", [(0, 1), (1, 0)])
     head = lax.axis_index("head").astype(jnp.int32).reshape(1)
     gates, weight = prepare(target, levels.T, down_weight, experts * SLOTS)
     other, gates, weight = lax.optimization_barrier((other, gates, weight))
     outputs = run_experts(head, own, other, weight)
-    back = lax.all_to_all(outputs, "exp", split_axis=0, concat_axis=0, tiled=True)
+    back = exchange(outputs)
     return combine(gates, back)
 
 

time: 203 us -> 200 us (0.985)
  the two profiles are of different devices: /device:TPU:34 before, /device:TPU:24 now
where the time goes in v6:
time: 200 us
  blocking collectives  182 us (91%)
  Pallas kernels  15 us (8%)
    all_to_all x2, blocking collectives, exchange(): lax.all_to_all(array, 'exp', split_axis=0, concat_axis=0, tiled=True, axi...  182 us
    pallas_call x1, Pallas kernels, route(): pl.pallas_call(functools.partial(route_kernel, experts=experts), out_shap...  4.76 us
    pallas_call x1, Pallas kernels, run_experts(): pl.pallas_call(expert_kernel, out_shape=jax.ShapeDtypeStruct((sources, SL...  4.23 us
  transfers between devices with their start and end apart: 1, of which 1 were waited for; matrix products, arithmetic and copies ran while one was open for 0% of the time, Pallas kernels for 1%

profile of v6, /device:TPU:24, one launch (start us, length us, event | category | flops | bytes accessed | tf_op | source)
XLA Modules:
  0.0 199.8 jit_solution(7843438660000443721)
XLA Ops:
  0.0 0.0 copy-start
  0.0 4.8 %route.1 = (bf16[2048,384]{1,0:T(8,128)(2,1)S(1)}, s32[8,256]{1,0:T(8,128)S(1)}) custom-call(s32[6,256]{1,0:T(8,128)} %bitcast.10, bf16[1536,384]{1,0:T(8,128)(2,1)} %bitcast.9), custom_call_target="tpu_custom_call" | custom-call | tf_op jit(solution)/shard_map/route/pallas_call | solution.py:75
  4.8 57.7 %all_to_all.10.own_ref = bf16[64,32,384]{2,1,0:T(8,128)(2,1)S(1)} all-to-all(bf16[64,32,384]{2,1,0:T(8,128)(2,1)S(1)} %bitcast.7), channel_id=1, replica_groups={{0,3,6,1,4,7,2,5,8,11,14,9,12,15,10,13,16,19,22,17,20,23,18,21,24,27,30..., dimensions={0} | all-to-all | bytes 3145728 | tf_op jit(solution)/shard_map/all_to_all | solution.py:27
  62.4 1.9 collective-permute-start
  64.4 0.0 copy-done
  64.4 2.1 %prepare.1 = (bf16[2,256,2048]{2,1,0:T(8,128)(2,1)S(1)}, bf16[2,768,1280]{2,1,0:T(8,128)(2,1)S(1)}) custom-call(s32[8,256]{1,0:T(8,128)S(1)} %get-tuple-element.13.target_ref, s32[6,256]{1,0:T(8,128)S(1)} %bitcast.8, bf16[2,768,1280]{2,1,0:T(8,128)(2,1)} %weight_hbm.1), custom_call_target="tpu_custom_call" | custom-call | flops 4194304 | bytes 8388608 | tf_op jit(solution)/shard_map/prepare/pallas_call | solution.py:177
  66.5 1.2 collective-permute-done.other_ref
  67.7 4.2 %experts.1 = bf16[64,16,2432]{2,1,0:T(8,128)(2,1)S(1)} custom-call(s32[1]{0:T(128)} %bitcast.5.head_ref, bf16[64,32,384]{2,1,0:T(8,128)(2,1)S(1)} %all_to_all.10.own_ref, bf16[64,32,384]{2,1,0:T(8,128)(2,1)S(1)} %collective-permute-done.other_ref, bf16[2,768,1280]{2,1,0:T(8,128)(2,1)S(1)} %get-tuple-element.18.weight_ref), custom_call_target="tpu_custom_call" | custom-call | flops 4026531840 | bytes 12582912 | tf_op jit(solution)/shard_map/experts/pallas_call | solution.py:137
  72.0 124.0 %all_to_all.11.back_ref = bf16[64,16,2432]{2,1,0:T(8,128)(2,1)S(1)} all-to-all(bf16[64,16,2432]{2,1,0:T(8,128)(2,1)S(1)} %experts.1), channel_id=1, replica_groups={{0,3,6,1,4,7,2,5,8,11,14,9,12,15,10,13,16,19,22,17,20,23,18,21,24,27,30..., dimensions={0} | all-to-all | bytes 9961472 | tf_op jit(solution)/shard_map/all_to_all | solution.py:27
  195.9 3.9 %combine.1 = bf16[256,1280]{1,0:T(8,128)(2,1)} custom-call(bf16[2,256,2048]{2,1,0:T(8,128)(2,1)S(1)} %get-tuple-element.16.gates_ref, bf16[64,16,2432]{2,1,0:T(8,128)(2,1)S(1)} %all_to_all.11.back_ref), custom_call_target="tpu_custom_call" | custom-call | tf_op jit(solution)/shard_map/combine/pallas_call | solution.py:223
Async XLA Ops:
  0.0 64.4 %copy-start = (s32[256,6]{0,1:T(8,128)S(1)}, s32[256,6]{0,1:T(8,128)}, u32[]{:S(2)}) copy-start(s32[256,6]{0,1:T(8,128)} %param.6) | copy-start | bytes 18436
  62.4 5.3 %collective-permute-start = (bf16[64,32,384]{2,1,0:T(8,128)(2,1)S(1)}, bf16[64,32,384]{2,1,0:T(8,128)(2,1)S(1)}, u32[]{:S(2)}, u32[]{:S(2)}) collective-permute-start(bf16[64,32,384]{2,1,0:T(8,128)(2,1)S(1)} %all_to_all.10.own_ref), channel_id=1, source_target_pairs={{0,64},{64,0},{1,65},{65,1},{2,66},{66,2},{3,67},{67,3},{4,68},{68... | collective-permute-start | bytes 4718600 | tf_op jit(solution)/shard_map/ppermute | solution.py:244

commit v7 on v6

--- a/solution.py
+++ b/solution.py
@@ -19,11 +19,12 @@
 
 def placed(expert):
     device, own = expert // 2, expert % 2
-    return (device // RING * RING + device * STRIDE % RING) * 2 + own
+    z, y = device // RING, device % RING
+    return (z * RING + (y + (RING - 1) * z) * STRIDE % RING) * 2 + own
 
 
 def exchange(array):
-    order = [z + y * STRIDE % RING for z in range(0, array.shape[0], RING) for y in range(RING)]
+    order = [z * RING + (z + y * STRIDE) % RING for z in range(RING) for y in range(RING)]
     return lax.all_to_all(
         array, "exp", split_axis=0, concat_axis=0, tiled=True, axis_index_groups=[order]
     )

time: 200 us -> 211 us (1.055)
  the two profiles are of different devices: /device:TPU:24 before, /device:TPU:42 now
where the time goes in v7:
time: 211 us
  blocking collectives  193 us (91%)
  Pallas kernels  15 us (7%)
    all_to_all x2, blocking collectives, exchange(): lax.all_to_all(array, 'exp', split_axis=0, concat_axis=0, tiled=True, axi...  193 us
    pallas_call x1, Pallas kernels, route(): pl.pallas_call(functools.partial(route_kernel, experts=experts), out_shap...  4.76 us
    pallas_call x1, Pallas kernels, run_experts(): pl.pallas_call(expert_kernel, out_shape=jax.ShapeDtypeStruct((sources, SL...  4.23 us
  transfers between devices with their start and end apart: 1, of which 1 were waited for; matrix products, arithmetic and copies ran while one was open for 0% of the time, Pallas kernels for 1%

profile of v7, /device:TPU:42, one launch (start us, length us, event | category | flops | bytes accessed | tf_op | source)
XLA Modules:
  0.0 210.7 jit_solution(1430134536519558913)
XLA Ops:
  0.0 0.0 copy-start
  0.0 4.8 %route.1 = (bf16[2048,384]{1,0:T(8,128)(2,1)S(1)}, s32[8,256]{1,0:T(8,128)S(1)}) custom-call(s32[6,256]{1,0:T(8,128)} %bitcast.10, bf16[1536,384]{1,0:T(8,128)(2,1)} %bitcast.9), custom_call_target="tpu_custom_call" | custom-call | tf_op jit(solution)/shard_map/route/pallas_call | solution.py:76
  4.8 56.6 %all_to_all.10.own_ref = bf16[64,32,384]{2,1,0:T(8,128)(2,1)S(1)} all-to-all(bf16[64,32,384]{2,1,0:T(8,128)(2,1)S(1)} %bitcast.7), channel_id=1, replica_groups={{0,3,6,1,4,7,2,5,9,12,15,10,13,8,11,14,18,21,16,19,22,17,20,23,27,30,25..., dimensions={0} | all-to-all | bytes 3145728 | tf_op jit(solution)/shard_map/all_to_all | solution.py:28
  61.4 1.9 collective-permute-start
  63.3 0.0 copy-done
  63.4 2.1 %prepare.1 = (bf16[2,256,2048]{2,1,0:T(8,128)(2,1)S(1)}, bf16[2,768,1280]{2,1,0:T(8,128)(2,1)S(1)}) custom-call(s32[8,256]{1,0:T(8,128)S(1)} %get-tuple-element.13.target_ref, s32[6,256]{1,0:T(8,128)S(1)} %bitcast.8, bf16[2,768,1280]{2,1,0:T(8,128)(2,1)} %weight_hbm.1), custom_call_target="tpu_custom_call" | custom-call | flops 4194304 | bytes 8388608 | tf_op jit(solution)/shard_map/prepare/pallas_call | solution.py:178
  65.5 1.2 collective-permute-done.other_ref
  66.7 4.2 %experts.1 = bf16[64,16,2432]{2,1,0:T(8,128)(2,1)S(1)} custom-call(s32[1]{0:T(128)} %bitcast.5.head_ref, bf16[64,32,384]{2,1,0:T(8,128)(2,1)S(1)} %all_to_all.10.own_ref, bf16[64,32,384]{2,1,0:T(8,128)(2,1)S(1)} %collective-permute-done.other_ref, bf16[2,768,1280]{2,1,0:T(8,128)(2,1)S(1)} %get-tuple-element.18.weight_ref), custom_call_target="tpu_custom_call" | custom-call | flops 4026531840 | bytes 12582912 | tf_op jit(solution)/shard_map/experts/pallas_call | solution.py:138
  71.0 135.9 %all_to_all.11.back_ref = bf16[64,16,2432]{2,1,0:T(8,128)(2,1)S(1)} all-to-all(bf16[64,16,2432]{2,1,0:T(8,128)(2,1)S(1)} %experts.1), channel_id=1, replica_groups={{0,3,6,1,4,7,2,5,9,12,15,10,13,8,11,14,18,21,16,19,22,17,20,23,27,30,25..., dimensions={0} | all-to-all | bytes 9961472 | tf_op jit(solution)/shard_map/all_to_all | solution.py:28
  206.8 3.9 %combine.1 = bf16[256,1280]{1,0:T(8,128)(2,1)} custom-call(bf16[2,256,2048]{2,1,0:T(8,128)(2,1)S(1)} %get-tuple-element.16.gates_ref, bf16[64,16,2432]{2,1,0:T(8,128)(2,1)S(1)} %all_to_all.11.back_ref), custom_call_target="tpu_custom_call" | custom-call | tf_op jit(solution)/shard_map/combine/pallas_call | solution.py:224
Async XLA Ops:
  0.0 63.3 %copy-start = (s32[256,6]{0,1:T(8,128)S(1)}, s32[256,6]{0,1:T(8,128)}, u32[]{:S(2)}) copy-start(s32[256,6]{0,1:T(8,128)} %param.6) | copy-start | bytes 18436
  61.4 5.3 %collective-permute-start = (bf16[64,32,384]{2,1,0:T(8,128)(2,1)S(1)}, bf16[64,32,384]{2,1,0:T(8,128)(2,1)S(1)}, u32[]{:S(2)}, u32[]{:S(2)}) collective-permute-start(bf16[64,32,384]{2,1,0:T(8,128)(2,1)S(1)} %all_to_all.10.own_ref), channel_id=1, source_target_pairs={{0,64},{64,0},{1,65},{65,1},{2,66},{66,2},{3,67},{67,3},{4,68},{68... | collective-permute-start | bytes 4718600 | tf_op jit(solution)/shard_map/ppermute | solution.py:245

commit v8 on v6

--- a/solution.py
+++ b/solution.py
@@ -189,44 +189,59 @@
     )(target, levels, far(weight))
 
 
-def combine_kernel(gates_ref, back_ref, out_ref):
+def combine_kernel(gates_ref, back_ref, out_far, out_ref, sems):
     sources, _, lanes = back_ref.shape
     width = out_ref.shape[1]
     rows = sources * SLOTS
     tile = 2 * LANES
+    parts = width // tile
     row = lax.broadcasted_iota(jnp.int32, (sources, SLOTS, LANES), 1)
     unfolded = jnp.zeros((sources, SLOTS, LANES), jnp.float32)
-    for j in range(SLOTS - 1):
-        block = back_ref[:, :, j * LANES : (j + 1) * LANES].astype(jnp.float32)
-        unfolded = jnp.where(row == j, block[:, SLOTS - 1 : SLOTS, :], unfolded)
-    unfolded = unfolded.astype(jnp.bfloat16).reshape(rows, LANES)
+    share = -(-(SLOTS - 1) // (parts - 1))
+    copies = []
 
     def gated(e, back):
         at = slice(e * rows, (e + 1) * rows)
         high = jnp.dot(gates_ref[0, :, at], back, preferred_element_type=jnp.float32)
         return high + jnp.dot(gates_ref[1, :, at], back, preferred_element_type=jnp.float32)
 
-    for n in range(0, width, tile):
-        first = back_ref[:, :, n : n + tile].reshape(rows, tile)
-        at = width + n
-        if at + tile <= lanes:
+    for n in range(parts):
+        first = back_ref[:, :, n * tile : (n + 1) * tile].reshape(rows, tile)
+        at = width + n * tile
+        if n < parts - 1:
             second = back_ref[:, :, at : at + tile].reshape(rows, tile)
         else:
             second = jnp.concatenate(
-                [back_ref[:, :, at : at + LANES].reshape(rows, LANES), unfolded], axis=1
+                [
+                    back_ref[:, :, at : at + LANES].reshape(rows, LANES),
+                    unfolded.astype(jnp.bfloat16).reshape(rows, LANES),
+                ],
+                axis=1,
             )
         total = gated(0, first) + gated(1, second)
-        out_ref[:, n : n + tile] = (total * (1.0 / 1024.0)).astype(jnp.bfloat16)
+        to = slice(n * tile, (n + 1) * tile)
+        out_ref[:, to] = (total * (1.0 / 1024.0)).astype(jnp.bfloat16)
+        copies.append(pltpu.make_async_copy(out_ref.at[:, to], out_far.at[:, to], sems.at[n]))
+        copies[n].start()
+        for j in range(n * share, min((n + 1) * share, SLOTS - 1)):
+            block = back_ref[:, :, j * LANES : (j + 1) * LANES].astype(jnp.float32)
+            unfolded = jnp.where(row == j, block[:, SLOTS - 1 : SLOTS, :], unfolded)
+    for copy in copies:
+        copy.wait()
 
 
 def combine(gates, back):
+    tokens = gates.shape[1]
+    width = (back.shape[2] + LANES) // 2
     return pl.pallas_call(
         combine_kernel,
-        out_shape=jax.ShapeDtypeStruct(
-            (gates.shape[1], (back.shape[2] + LANES) // 2), jnp.bfloat16
-        ),
+        out_shape=jax.ShapeDtypeStruct((tokens, width), jnp.bfloat16),
         in_specs=[WHOLE, WHOLE],
-        out_specs=WHOLE,
+        out_specs=FAR,
+        scratch_shapes=[
+            pltpu.VMEM((tokens, width), jnp.bfloat16),
+            pltpu.SemaphoreType.DMA((width // (2 * LANES),)),
+        ],
         compiler_params=pltpu.CompilerParams(vmem_limit_bytes=VMEM),
         name="combine",
     )(gates, back)

time: 200 us -> 200 us (level)
  no operation moved by 1% of the time
where the time goes in v8:
time: 200 us
  blocking collectives  182 us (91%)
  Pallas kernels  14.9 us (7%)
    all_to_all x2, blocking collectives, exchange(): lax.all_to_all(array, 'exp', split_axis=0, concat_axis=0, tiled=True, axi...  182 us
    pallas_call x1, Pallas kernels, route(): pl.pallas_call(functools.partial(route_kernel, experts=experts), out_shap...  4.76 us
    pallas_call x1, Pallas kernels, run_experts(): pl.pallas_call(expert_kernel, out_shape=jax.ShapeDtypeStruct((sources, SL...  4.23 us
  transfers between devices with their start and end apart: 1, of which 1 were waited for; matrix products, arithmetic and copies ran while one was open for 0% of the time, Pallas kernels for 1%

profile of v8, /device:TPU:24, one launch (start us, length us, event | category | flops | bytes accessed | tf_op | source)
XLA Modules:
  0.0 199.7 jit_solution(2790192815980207553)
XLA Ops:
  0.0 0.0 copy-start
  0.0 4.8 %route.1 = (bf16[2048,384]{1,0:T(8,128)(2,1)S(1)}, s32[8,256]{1,0:T(8,128)S(1)}) custom-call(s32[6,256]{1,0:T(8,128)} %bitcast.10, bf16[1536,384]{1,0:T(8,128)(2,1)} %bitcast.9), custom_call_target="tpu_custom_call" | custom-call | tf_op jit(solution)/shard_map/route/pallas_call | solution.py:75
  4.8 57.7 %all_to_all.10.own_ref = bf16[64,32,384]{2,1,0:T(8,128)(2,1)S(1)} all-to-all(bf16[64,32,384]{2,1,0:T(8,128)(2,1)S(1)} %bitcast.7), channel_id=1, replica_groups={{0,3,6,1,4,7,2,5,8,11,14,9,12,15,10,13,16,19,22,17,20,23,18,21,24,27,30..., dimensions={0} | all-to-all | bytes 3145728 | tf_op jit(solution)/shard_map/all_to_all | solution.py:27
  62.4 1.9 collective-permute-start
  64.4 0.0 copy-done
  64.4 2.1 %prepare.1 = (bf16[2,256,2048]{2,1,0:T(8,128)(2,1)S(1)}, bf16[2,768,1280]{2,1,0:T(8,128)(2,1)S(1)}) custom-call(s32[8,256]{1,0:T(8,128)S(1)} %get-tuple-element.13.target_ref, s32[6,256]{1,0:T(8,128)S(1)} %bitcast.8, bf16[2,768,1280]{2,1,0:T(8,128)(2,1)} %weight_hbm.1), custom_call_target="tpu_custom_call" | custom-call | flops 4194304 | bytes 8388608 | tf_op jit(solution)/shard_map/prepare/pallas_call | solution.py:177
  66.5 1.2 collective-permute-done.other_ref
  67.7 4.2 %experts.1 = bf16[64,16,2432]{2,1,0:T(8,128)(2,1)S(1)} custom-call(s32[1]{0:T(128)} %bitcast.5.head_ref, bf16[64,32,384]{2,1,0:T(8,128)(2,1)S(1)} %all_to_all.10.own_ref, bf16[64,32,384]{2,1,0:T(8,128)(2,1)S(1)} %collective-permute-done.other_ref, bf16[2,768,1280]{2,1,0:T(8,128)(2,1)S(1)} %get-tuple-element.18.weight_ref), custom_call_target="tpu_custom_call" | custom-call | flops 4026531840 | bytes 12582912 | tf_op jit(solution)/shard_map/experts/pallas_call | solution.py:137
  72.0 124.0 %all_to_all.11.back_ref = bf16[64,16,2432]{2,1,0:T(8,128)(2,1)S(1)} all-to-all(bf16[64,16,2432]{2,1,0:T(8,128)(2,1)S(1)} %experts.1), channel_id=1, replica_groups={{0,3,6,1,4,7,2,5,8,11,14,9,12,15,10,13,16,19,22,17,20,23,18,21,24,27,30..., dimensions={0} | all-to-all | bytes 9961472 | tf_op jit(solution)/shard_map/all_to_all | solution.py:27
  195.9 3.8 %combine.1 = bf16[256,1280]{1,0:T(8,128)(2,1)} custom-call(bf16[2,256,2048]{2,1,0:T(8,128)(2,1)S(1)} %get-tuple-element.16.gates_ref, bf16[64,16,2432]{2,1,0:T(8,128)(2,1)S(1)} %all_to_all.11.back_ref), custom_call_target="tpu_custom_call" | custom-call | tf_op jit(solution)/shard_map/combine/pallas_call | solution.py:236
Async XLA Ops:
  0.0 64.4 %copy-start = (s32[256,6]{0,1:T(8,128)S(1)}, s32[256,6]{0,1:T(8,128)}, u32[]{:S(2)}) copy-start(s32[256,6]{0,1:T(8,128)} %param.6) | copy-start | bytes 18436
  62.4 5.3 %collective-permute-start = (bf16[64,32,384]{2,1,0:T(8,128)(2,1)S(1)}, bf16[64,32,384]{2,1,0:T(8,128)(2,1)S(1)}, u32[]{:S(2)}, u32[]{:S(2)}) collective-permute-start(bf16[64,32,384]{2,1,0:T(8,128)(2,1)S(1)} %all_to_all.10.own_ref), channel_id=1, source_target_pairs={{0,64},{64,0},{1,65},{65,1},{2,66},{66,2},{3,67},{67,3},{4,68},{68... | collective-permute-start | bytes 4718600 | tf_op jit(solution)/shard_map/ppermute | solution.py:259
